TPU v7x, 256 devices: a whole 4x4x8 slice. The times are simulated.
256 devices in a mesh: probe: 2 (over x_hi), gx: 16 (over z, core), gy: 8 (over y, x_lo).
Axes of the slice: x: 4 (x_hi: 2, x_lo: 2; x = x_hi * 2 + x_lo), y: 4, z: 8, core: 2. Of those that a mesh axis runs over, the one named last changes fastest.
Arguments:
- probes: float32 [8, 1024, 1024], P('probe', 'gx', 'gy'), may hold values from -6 to 6
- base_velocity: float32 [2, 1024, 1024], P(None, 'gx', 'gy'), may hold values from -6 to 6
- viscosity: float32 [1024, 1024], P('gx', 'gy'), may hold values from 0.1 to 0.4
- friction: float32 [1024, 1024], P('gx', 'gy'), may hold values from 0.25 to 1
- noise_weight: float32 [1024, 1024], P('gx', 'gy'), may hold values from 1 to 16
- ice_mask: int32 [1024, 1024], P('gx', 'gy'), may hold values 0 or 1
Outputs:
- images: float32 [8, 1024, 1024], P('probe', 'gx', 'gy')
- factor: float32 [8, 1024, 1024], P('probe', 'gx', 'gy')
- gram: float32 [8, 8], replicated
All inputs are finite; a program needn't handle non-finite values. No bound on the sum of `ice_mask` on one device may be relied on, other than what follows from the above.
Results may differ from a plain program's by a relative error of at most 0.000082.
Values sent between devices are 32-bit elements; how exact they have to be, the bound alone decides.
A program may use at most 64 MiB of HBM per device.

v0:
```python
import jax
import jax.numpy as jnp
from jax import lax
from jax.sharding import PartitionSpec as P

SWEEPS = 9
OMEGA = 0.6
DRAG = 0.05
PRIOR = 0.05


def extended(x, sides, width):
    for axis, dim in sides:
        size, length = (lax.axis_size(axis), x.shape[dim])
        up = [(i, (i + 1) % size) for i in range(size - 1)]
        down = [(j, i) for i, j in up]
        last = lax.slice_in_dim(x, length - width, length, axis=dim)
        first = lax.slice_in_dim(x, 0, width, axis=dim)
        before = lax.ppermute(last, axis, up)
        after = lax.ppermute(first, axis, down)
        x = jnp.concatenate([before, x, after], axis=dim)
    return x


def near(values, step_x, step_y):
    row_count = values.shape[-2]
    column_count = values.shape[-1]
    return values[..., 1 + step_x : row_count - 1 + step_x, 1 + step_y : column_count - 1 + step_y]


def diagonal_of(eta_pad, react):
    eta_mid = near(eta_pad, 0, 0)
    sum_first = near(eta_pad, 1, 0) + near(eta_pad, -1, 0)
    sum_second = near(eta_pad, 0, 1) + near(eta_pad, 0, -1)
    first = 2.0 * (2.0 * eta_mid + sum_first) + 0.5 * (2.0 * eta_mid + sum_second) + react
    second = 0.5 * (2.0 * eta_mid + sum_first) + 2.0 * (2.0 * eta_mid + sum_second) + react
    return jnp.stack([first, second], axis=-3)


def stencil(field_pad, eta_pad, react):
    eta_mid = near(eta_pad, 0, 0)
    eta_east = near(eta_pad, 1, 0)
    eta_west = near(eta_pad, -1, 0)
    eta_north = near(eta_pad, 0, 1)
    eta_south = near(eta_pad, 0, -1)
    along_x = field_pad[..., 0, :, :]
    along_y = field_pad[..., 1, :, :]
    x_mid = near(along_x, 0, 0)
    x_east = near(along_x, 1, 0)
    x_west = near(along_x, -1, 0)
    x_north = near(along_x, 0, 1)
    x_south = near(along_x, 0, -1)
    x_northeast = near(along_x, 1, 1)
    x_southeast = near(along_x, 1, -1)
    x_northwest = near(along_x, -1, 1)
    x_southwest = near(along_x, -1, -1)
    y_mid = near(along_y, 0, 0)
    y_east = near(along_y, 1, 0)
    y_west = near(along_y, -1, 0)
    y_north = near(along_y, 0, 1)
    y_south = near(along_y, 0, -1)
    y_northeast = near(along_y, 1, 1)
    y_southeast = near(along_y, 1, -1)
    y_northwest = near(along_y, -1, 1)
    y_southwest = near(along_y, -1, -1)
    first = (
        2.0 * (eta_mid + eta_east) * (x_mid - x_east)
        + 2.0 * (eta_mid + eta_west) * (x_mid - x_west)
        + 0.5 * (eta_mid + eta_north) * (x_mid - x_north)
        + 0.5 * (eta_mid + eta_south) * (x_mid - x_south)
        - 0.5 * (eta_east * (y_northeast - y_southeast) - eta_west * (y_northwest - y_southwest))
        - 0.25 * (eta_north * (y_northeast - y_northwest) - eta_south * (y_southeast - y_southwest))
        + react * x_mid
    )
    second = (
        0.5 * (eta_mid + eta_east) * (y_mid - y_east)
        + 0.5 * (eta_mid + eta_west) * (y_mid - y_west)
        + 2.0 * (eta_mid + eta_north) * (y_mid - y_north)
        + 2.0 * (eta_mid + eta_south) * (y_mid - y_south)
        - 0.5 * (eta_north * (x_northeast - x_northwest) - eta_south * (x_southeast - x_southwest))
        - 0.25 * (eta_east * (x_northeast - x_southeast) - eta_west * (x_northwest - x_southwest))
        + react * y_mid
    )
    return jnp.stack([first, second], axis=-3)


def body(probes, base_velocity, viscosity, friction, noise_weight, ice_mask):
    ice = ice_mask.astype(jnp.float32)
    coupling = friction * ice
    react = coupling + DRAG
    eta_pad = extended(viscosity, (("gx", 0), ("gy", 1)), 1)
    diag = diagonal_of(eta_pad, react)

    def relax(source):
        state = OMEGA * source / diag
        for sweep in range(SWEEPS - 1):
            padded = extended(state, (("gx", 2), ("gy", 3)), 1)
            state = state + OMEGA * (source - stencil(padded, eta_pad, react)) / diag
        return state

    source = (-coupling * base_velocity)[None] * probes[:, None]
    response = relax(source)
    adjoint = relax(noise_weight * response)
    images = -coupling * jnp.sum(base_velocity * adjoint, axis=1) + PRIOR * probes
    gathered = lax.all_gather(images, "probe", axis=0, tiled=True)
    probe_total = gathered.shape[0]
    flat_probes = probes.reshape(probes.shape[0], -1)
    flat_images = gathered.reshape(probe_total, -1)
    partial_rows = jnp.dot(flat_probes, flat_images.T, precision=lax.Precision.HIGHEST)
    total_cells = float(
        viscosity.shape[0] * lax.axis_size("gx") * viscosity.shape[1] * lax.axis_size("gy")
    )
    start = lax.axis_index("probe") * probes.shape[0]
    placed = lax.dynamic_update_slice(
        jnp.zeros((probe_total, probe_total), jnp.float32), partial_rows, (start, 0)
    )
    gram = lax.psum(placed, ("probe", "gx", "gy")) / total_cells
    lower = jnp.linalg.cholesky(gram)
    solved = jax.scipy.linalg.solve_triangular(lower, flat_images, lower=True)
    factor = lax.dynamic_slice_in_dim(solved, start, probes.shape[0], 0).reshape(probes.shape)
    return (images, factor, gram)


def solution(mesh):
    in_specs = (
        P("probe", "gx", "gy"),
        P(None, "gx", "gy"),
        P("gx", "gy"),
        P("gx", "gy"),
        P("gx", "gy"),
        P("gx", "gy"),
    )
    out_specs = (P("probe", "gx", "gy"), P("probe", "gx", "gy"), P())
    return jax.shard_map(body, mesh=mesh, in_specs=in_specs, out_specs=out_specs, check_vma=False)
```

profile of v0, /device:TPU:1, one launch (start us, length us, event | category | flops | bytes accessed | tf_op | source)
XLA Modules:
  0.0 494.4 jit_solution(14787006086745405829)
XLA Ops:
  1.3 5.1 %collective-permute-start = (f32[1,128]{1,0:T(1,128)S(1)}, f32[1,128]{1,0:T(1,128)S(1)}, u32[]{:S(2)}, u32[]{:S(2)}) collective-permute-start(f32[1,128]{1,0:T(1,128)S(1)} %get-tuple-element.130), channel_id=1, source_target_pairs={{8,0},{16,8},{24,16},{32,24},{40,32},{48,40},{56,48},{64,56},{72,6... | collective-permute-start | bytes 1544 | tf_op jit(solution)/shard_map/ppermute | solution.py:20
  18.7 4.9 collective-permute-start.4
  34.0 4.1 collective-permute-done.6
  38.1 9.6 %collective-permute-done.7 = f32[4,2,66,1]{3,2,0,1:T(8,128)S(1)} collective-permute-done((f32[4,2,66,1]{3,2,0,1:T(8,128)S(1)}, f32[4,2,66,1]{3,2,0,1:T(8,128)S(1)}, u32[]{:S(2)}, u32[]{:S(2)}) %collective-permute-start.7) | collective-permute-done | bytes 2144 | tf_op jit(solution)/shard_map/ppermute | solution.py:20
  59.9 4.1 collective-permute-done.10
  64.0 9.8 %collective-permute-done.11 = f32[4,2,66,1]{3,2,0,1:T(8,128)S(1)} collective-permute-done((f32[4,2,66,1]{3,2,0,1:T(8,128)S(1)}, f32[4,2,66,1]{3,2,0,1:T(8,128)S(1)}, u32[]{:S(2)}, u32[]{:S(2)}) %collective-permute-start.11) | collective-permute-done | bytes 2144 | tf_op jit(solution)/shard_map/ppermute | solution.py:20
  86.4 4.1 collective-permute-done.14
  90.5 9.8 %collective-permute-done.15 = f32[4,2,66,1]{3,2,0,1:T(8,128)S(1)} collective-permute-done((f32[4,2,66,1]{3,2,0,1:T(8,128)S(1)}, f32[4,2,66,1]{3,2,0,1:T(8,128)S(1)}, u32[]{:S(2)}, u32[]{:S(2)}) %collective-permute-start.15) | collective-permute-done | bytes 2144 | tf_op jit(solution)/shard_map/ppermute | solution.py:20
  101.4 4.5 collective-permute-start.16
  117.6 6.5 %collective-permute-done.19 = f32[4,2,66,1]{3,2,0,1:T(8,128)S(1)} collective-permute-done((f32[4,2,66,1]{3,2,0,1:T(8,128)S(1)}, f32[4,2,66,1]{3,2,0,1:T(8,128)S(1)}, u32[]{:S(2)}, u32[]{:S(2)}) %collective-permute-start.19) | collective-permute-done | bytes 2144 | tf_op jit(solution)/shard_map/ppermute | solution.py:20
  136.6 4.1 collective-permute-done.22
  140.7 6.5 %collective-permute-done.23 = f32[4,2,66,1]{3,2,0,1:T(8,128)S(1)} collective-permute-done((f32[4,2,66,1]{3,2,0,1:T(8,128)S(1)}, f32[4,2,66,1]{3,2,0,1:T(8,128)S(1)}, u32[]{:S(2)}, u32[]{:S(2)}) %collective-permute-start.23) | collective-permute-done | bytes 2144 | tf_op jit(solution)/shard_map/ppermute | solution.py:20
  148.4 4.2 collective-permute-start.24
  161.0 4.1 collective-permute-done.26
  165.1 6.5 %collective-permute-done.27 = f32[4,2,66,1]{3,2,0,1:T(8,128)S(1)} collective-permute-done((f32[4,2,66,1]{3,2,0,1:T(8,128)S(1)}, f32[4,2,66,1]{3,2,0,1:T(8,128)S(1)}, u32[]{:S(2)}, u32[]{:S(2)}) %collective-permute-start.27) | collective-permute-done | bytes 2144 | tf_op jit(solution)/shard_map/ppermute | solution.py:20
  189.4 6.5 %collective-permute-done.31 = f32[4,2,66,1]{3,2,0,1:T(8,128)S(1)} collective-permute-done((f32[4,2,66,1]{3,2,0,1:T(8,128)S(1)}, f32[4,2,66,1]{3,2,0,1:T(8,128)S(1)}, u32[]{:S(2)}, u32[]{:S(2)}) %collective-permute-start.31) | collective-permute-done | bytes 2144 | tf_op jit(solution)/shard_map/ppermute | solution.py:20
  209.4 4.1 collective-permute-done.34
  213.5 6.5 %collective-permute-done.35 = f32[4,2,66,1]{3,2,0,1:T(8,128)S(1)} collective-permute-done((f32[4,2,66,1]{3,2,0,1:T(8,128)S(1)}, f32[4,2,66,1]{3,2,0,1:T(8,128)S(1)}, u32[]{:S(2)}, u32[]{:S(2)}) %collective-permute-start.35) | collective-permute-done | bytes 2144 | tf_op jit(solution)/shard_map/ppermute | solution.py:20
  233.6 4.1 collective-permute-done.38
  237.7 6.5 %collective-permute-done.39 = f32[4,2,66,1]{3,2,0,1:T(8,128)S(1)} collective-permute-done((f32[4,2,66,1]{3,2,0,1:T(8,128)S(1)}, f32[4,2,66,1]{3,2,0,1:T(8,128)S(1)}, u32[]{:S(2)}, u32[]{:S(2)}) %collective-permute-start.39) | collective-permute-done | bytes 2144 | tf_op jit(solution)/shard_map/ppermute | solution.py:20
  256.6 4.1 collective-permute-done.42
  260.7 6.5 %collective-permute-done.43 = f32[4,2,66,1]{3,2,0,1:T(8,128)S(1)} collective-permute-done((f32[4,2,66,1]{3,2,0,1:T(8,128)S(1)}, f32[4,2,66,1]{3,2,0,1:T(8,128)S(1)}, u32[]{:S(2)}, u32[]{:S(2)}) %collective-permute-start.43) | collective-permute-done | bytes 2144 | tf_op jit(solution)/shard_map/ppermute | solution.py:20
  279.4 4.1 collective-permute-done.46
  283.5 6.5 %collective-permute-done.47 = f32[4,2,66,1]{3,2,0,1:T(8,128)S(1)} collective-permute-done((f32[4,2,66,1]{3,2,0,1:T(8,128)S(1)}, f32[4,2,66,1]{3,2,0,1:T(8,128)S(1)}, u32[]{:S(2)}, u32[]{:S(2)}) %collective-permute-start.47) | collective-permute-done | bytes 2144 | tf_op jit(solution)/shard_map/ppermute | solution.py:20
  302.3 4.1 collective-permute-done.50
  306.4 6.5 %collective-permute-done.51 = f32[4,2,66,1]{3,2,0,1:T(8,128)S(1)} collective-permute-done((f32[4,2,66,1]{3,2,0,1:T(8,128)S(1)}, f32[4,2,66,1]{3,2,0,1:T(8,128)S(1)}, u32[]{:S(2)}, u32[]{:S(2)}) %collective-permute-start.51) | collective-permute-done | bytes 2144 | tf_op jit(solution)/shard_map/ppermute | solution.py:20
  329.4 6.5 %collective-permute-done.55 = f32[4,2,66,1]{3,2,0,1:T(8,128)S(1)} collective-permute-done((f32[4,2,66,1]{3,2,0,1:T(8,128)S(1)}, f32[4,2,66,1]{3,2,0,1:T(8,128)S(1)}, u32[]{:S(2)}, u32[]{:S(2)}) %collective-permute-start.55) | collective-permute-done | bytes 2144 | tf_op jit(solution)/shard_map/ppermute | solution.py:20
  353.3 6.5 %collective-permute-done.59 = f32[4,2,66,1]{3,2,0,1:T(8,128)S(1)} collective-permute-done((f32[4,2,66,1]{3,2,0,1:T(8,128)S(1)}, f32[4,2,66,1]{3,2,0,1:T(8,128)S(1)}, u32[]{:S(2)}, u32[]{:S(2)}) %collective-permute-start.59) | collective-permute-done | bytes 2144 | tf_op jit(solution)/shard_map/ppermute | solution.py:20
  376.8 6.5 %collective-permute-done.63 = f32[4,2,66,1]{3,2,0,1:T(8,128)S(1)} collective-permute-done((f32[4,2,66,1]{3,2,0,1:T(8,128)S(1)}, f32[4,2,66,1]{3,2,0,1:T(8,128)S(1)}, u32[]{:S(2)}, u32[]{:S(2)}) %collective-permute-start.63) | collective-permute-done | bytes 2144 | tf_op jit(solution)/shard_map/ppermute | solution.py:20
  399.8 6.5 %collective-permute-done.67 = f32[4,2,66,1]{3,2,1,0:T(8,128)S(1)} collective-permute-done((f32[4,2,66,1]{3,2,1,0:T(8,128)S(1)}, f32[4,2,66,1]{3,2,1,0:T(8,128)S(1)}, u32[]{:S(2)}, u32[]{:S(2)}) %collective-permute-start.67) | collective-permute-done | bytes 2144 | tf_op jit(solution)/shard_map/ppermute | solution.py:20
  407.4 6.8 %all_gather.3 = f32[8,64,128]{2,1,0:T(8,128)S(1)} all-gather(f32[4,64,128]{2,1,0:T(8,128)S(1)} %multiply_add_fusion), channel_id=1, replica_groups=mesh['probe'=2,'gx'=16,'gy'=8] {'probe'}, dimensions={0}, use_global_device_ids=true | all-gather | bytes 393216 | tf_op jit(solution)/shard_map/all_gather | solution.py:105
  415.1 74.6 %psum.7 = f32[8,8]{0,1:T(8,128)S(1)} all-reduce(f32[8,8]{0,1:T(8,128)S(1)} %dynamic_update_slice.3), channel_id=1, replica_groups=mesh['probe'=2,'gx'=16,'gy'=8] {'probe','gx','gy'}, use_global_device_ids=true, to_apply=%region_1.0 | all-reduce | flops 64 | bytes 512 | tf_op jit(solution)/shard_map/psum | solution.py:117
  (275 shorter events, 237.5 us)
Async XLA Ops:
  1.3 7.1 %collective-permute-start = (f32[1,128]{1,0:T(1,128)S(1)}, f32[1,128]{1,0:T(1,128)S(1)}, u32[]{:S(2)}, u32[]{:S(2)}) collective-permute-start(f32[1,128]{1,0:T(1,128)S(1)} %get-tuple-element.130), channel_id=1, source_target_pairs={{8,0},{16,8},{24,16},{32,24},{40,32},{48,40},{56,48},{64,56},{72,6... | collective-permute-start | bytes 1544 | tf_op jit(solution)/shard_map/ppermute | solution.py:20
  18.7 6.8 %collective-permute-start.4 = (f32[4,2,1,128]{3,2,0,1:T(1,128)S(1)}, f32[4,2,1,128]{3,2,0,1:T(1,128)S(1)}, u32[]{:S(2)}, u32[]{:S(2)}) collective-permute-start(f32[4,2,1,128]{3,2,0,1:T(1,128)S(1)} %get-tuple-element.114), channel_id=1, source_target_pairs={{0,8},{8,16},{16,24},{24,32},{32,40},{40,48},{48,56},{56,64},{64,7... | collective-permute-start | bytes 12296 | tf_op jit(solution)/shard_map/ppermute | solution.py:19
  28.7 9.4 %collective-permute-start.6 = (f32[4,2,66,1]{3,2,0,1:T(8,128)S(1)}, f32[4,2,66,1]{3,2,0,1:T(8,128)S(1)}, u32[]{:S(2)}, u32[]{:S(2)}) collective-permute-start(f32[4,2,66,1]{3,2,0,1:T(8,128)S(1)} %get-tuple-element.82), channel_id=1, source_target_pairs={{0,1},{1,2},{2,3},{3,4},{4,5},{5,6},{6,7},{8,9},{9,10},{10,11},{11... | collective-permute-start | bytes 6344 | tf_op jit(solution)/shard_map/ppermute | solution.py:19
  32.7 15.0 %collective-permute-start.7 = (f32[4,2,66,1]{3,2,0,1:T(8,128)S(1)}, f32[4,2,66,1]{3,2,0,1:T(8,128)S(1)}, u32[]{:S(2)}, u32[]{:S(2)}) collective-permute-start(f32[4,2,66,1]{3,2,0,1:T(8,128)S(1)} %get-tuple-element.83), channel_id=1, source_target_pairs={{1,0},{2,1},{3,2},{4,3},{5,4},{6,5},{7,6},{9,8},{10,9},{11,10},{12... | collective-permute-start | bytes 6344 | tf_op jit(solution)/shard_map/ppermute | solution.py:20
  58.6 15.2 %collective-permute-start.11 = (f32[4,2,66,1]{3,2,0,1:T(8,128)S(1)}, f32[4,2,66,1]{3,2,0,1:T(8,128)S(1)}, u32[]{:S(2)}, u32[]{:S(2)}) collective-permute-start(f32[4,2,66,1]{3,2,0,1:T(8,128)S(1)} %get-tuple-element.81), channel_id=1, source_target_pairs={{1,0},{2,1},{3,2},{4,3},{5,4},{6,5},{7,6},{9,8},{10,9},{11,10},{12... | collective-permute-start | bytes 6344 | tf_op jit(solution)/shard_map/ppermute | solution.py:20
  83.7 6.7 %collective-permute-start.14 = (f32[4,2,66,1]{3,2,0,1:T(8,128)S(1)}, f32[4,2,66,1]{3,2,0,1:T(8,128)S(1)}, u32[]{:S(2)}, u32[]{:S(2)}) collective-permute-start(f32[4,2,66,1]{3,2,0,1:T(8,128)S(1)} %get-tuple-element.78), channel_id=1, source_target_pairs={{0,1},{1,2},{2,3},{3,4},{4,5},{5,6},{6,7},{8,9},{9,10},{10,11},{11... | collective-permute-start | bytes 6344 | tf_op jit(solution)/shard_map/ppermute | solution.py:19
  85.1 15.2 %collective-permute-start.15 = (f32[4,2,66,1]{3,2,0,1:T(8,128)S(1)}, f32[4,2,66,1]{3,2,0,1:T(8,128)S(1)}, u32[]{:S(2)}, u32[]{:S(2)}) collective-permute-start(f32[4,2,66,1]{3,2,0,1:T(8,128)S(1)} %get-tuple-element.79), channel_id=1, source_target_pairs={{1,0},{2,1},{3,2},{4,3},{5,4},{6,5},{7,6},{9,8},{10,9},{11,10},{12... | collective-permute-start | bytes 6344 | tf_op jit(solution)/shard_map/ppermute | solution.py:20
  112.3 11.8 %collective-permute-start.19 = (f32[4,2,66,1]{3,2,0,1:T(8,128)S(1)}, f32[4,2,66,1]{3,2,0,1:T(8,128)S(1)}, u32[]{:S(2)}, u32[]{:S(2)}) collective-permute-start(f32[4,2,66,1]{3,2,0,1:T(8,128)S(1)} %get-tuple-element.77), channel_id=1, source_target_pairs={{1,0},{2,1},{3,2},{4,3},{5,4},{6,5},{7,6},{9,8},{10,9},{11,10},{12... | collective-permute-start | bytes 6344 | tf_op jit(solution)/shard_map/ppermute | solution.py:20
  133.3 7.4 %collective-permute-start.22 = (f32[4,2,66,1]{3,2,0,1:T(8,128)S(1)}, f32[4,2,66,1]{3,2,0,1:T(8,128)S(1)}, u32[]{:S(2)}, u32[]{:S(2)}) collective-permute-start(f32[4,2,66,1]{3,2,0,1:T(8,128)S(1)} %get-tuple-element.74), channel_id=1, source_target_pairs={{0,1},{1,2},{2,3},{3,4},{4,5},{5,6},{6,7},{8,9},{9,10},{10,11},{11... | collective-permute-start | bytes 6344 | tf_op jit(solution)/shard_map/ppermute | solution.py:19
  135.3 11.9 %collective-permute-start.23 = (f32[4,2,66,1]{3,2,0,1:T(8,128)S(1)}, f32[4,2,66,1]{3,2,0,1:T(8,128)S(1)}, u32[]{:S(2)}, u32[]{:S(2)}) collective-permute-start(f32[4,2,66,1]{3,2,0,1:T(8,128)S(1)} %get-tuple-element.75), channel_id=1, source_target_pairs={{1,0},{2,1},{3,2},{4,3},{5,4},{6,5},{7,6},{9,8},{10,9},{11,10},{12... | collective-permute-start | bytes 6344 | tf_op jit(solution)/shard_map/ppermute | solution.py:20
  157.7 7.4 %collective-permute-start.26 = (f32[4,2,66,1]{3,2,0,1:T(8,128)S(1)}, f32[4,2,66,1]{3,2,0,1:T(8,128)S(1)}, u32[]{:S(2)}, u32[]{:S(2)}) collective-permute-start(f32[4,2,66,1]{3,2,0,1:T(8,128)S(1)} %get-tuple-element.72), channel_id=1, source_target_pairs={{0,1},{1,2},{2,3},{3,4},{4,5},{5,6},{6,7},{8,9},{9,10},{10,11},{11... | collective-permute-start | bytes 6344 | tf_op jit(solution)/shard_map/ppermute | solution.py:19
  159.7 11.9 %collective-permute-start.27 = (f32[4,2,66,1]{3,2,0,1:T(8,128)S(1)}, f32[4,2,66,1]{3,2,0,1:T(8,128)S(1)}, u32[]{:S(2)}, u32[]{:S(2)}) collective-permute-start(f32[4,2,66,1]{3,2,0,1:T(8,128)S(1)} %get-tuple-element.73), channel_id=1, source_target_pairs={{1,0},{2,1},{3,2},{4,3},{5,4},{6,5},{7,6},{9,8},{10,9},{11,10},{12... | collective-permute-start | bytes 6344 | tf_op jit(solution)/shard_map/ppermute | solution.py:20
  182.0 7.4 %collective-permute-start.30 = (f32[4,2,66,1]{3,2,0,1:T(8,128)S(1)}, f32[4,2,66,1]{3,2,0,1:T(8,128)S(1)}, u32[]{:S(2)}, u32[]{:S(2)}) collective-permute-start(f32[4,2,66,1]{3,2,0,1:T(8,128)S(1)} %get-tuple-element.70), channel_id=1, source_target_pairs={{0,1},{1,2},{2,3},{3,4},{4,5},{5,6},{6,7},{8,9},{9,10},{10,11},{11... | collective-permute-start | bytes 6344 | tf_op jit(solution)/shard_map/ppermute | solution.py:19
  184.0 11.9 %collective-permute-start.31 = (f32[4,2,66,1]{3,2,0,1:T(8,128)S(1)}, f32[4,2,66,1]{3,2,0,1:T(8,128)S(1)}, u32[]{:S(2)}, u32[]{:S(2)}) collective-permute-start(f32[4,2,66,1]{3,2,0,1:T(8,128)S(1)} %get-tuple-element.71), channel_id=1, source_target_pairs={{1,0},{2,1},{3,2},{4,3},{5,4},{6,5},{7,6},{9,8},{10,9},{11,10},{12... | collective-permute-start | bytes 6344 | tf_op jit(solution)/shard_map/ppermute | solution.py:20
  206.1 7.4 %collective-permute-start.34 = (f32[4,2,66,1]{3,2,0,1:T(8,128)S(1)}, f32[4,2,66,1]{3,2,0,1:T(8,128)S(1)}, u32[]{:S(2)}, u32[]{:S(2)}) collective-permute-start(f32[4,2,66,1]{3,2,0,1:T(8,128)S(1)} %get-tuple-element.68), channel_id=1, source_target_pairs={{0,1},{1,2},{2,3},{3,4},{4,5},{5,6},{6,7},{8,9},{9,10},{10,11},{11... | collective-permute-start | bytes 6344 | tf_op jit(solution)/shard_map/ppermute | solution.py:19
  208.1 11.9 %collective-permute-start.35 = (f32[4,2,66,1]{3,2,0,1:T(8,128)S(1)}, f32[4,2,66,1]{3,2,0,1:T(8,128)S(1)}, u32[]{:S(2)}, u32[]{:S(2)}) collective-permute-start(f32[4,2,66,1]{3,2,0,1:T(8,128)S(1)} %get-tuple-element.69), channel_id=1, source_target_pairs={{1,0},{2,1},{3,2},{4,3},{5,4},{6,5},{7,6},{9,8},{10,9},{11,10},{12... | collective-permute-start | bytes 6344 | tf_op jit(solution)/shard_map/ppermute | solution.py:20
  230.3 7.4 %collective-permute-start.38 = (f32[4,2,66,1]{3,2,0,1:T(8,128)S(1)}, f32[4,2,66,1]{3,2,0,1:T(8,128)S(1)}, u32[]{:S(2)}, u32[]{:S(2)}) collective-permute-start(f32[4,2,66,1]{3,2,0,1:T(8,128)S(1)} %get-tuple-element.66), channel_id=1, source_target_pairs={{0,1},{1,2},{2,3},{3,4},{4,5},{5,6},{6,7},{8,9},{9,10},{10,11},{11... | collective-permute-start | bytes 6344 | tf_op jit(solution)/shard_map/ppermute | solution.py:19
  232.3 11.9 %collective-permute-start.39 = (f32[4,2,66,1]{3,2,0,1:T(8,128)S(1)}, f32[4,2,66,1]{3,2,0,1:T(8,128)S(1)}, u32[]{:S(2)}, u32[]{:S(2)}) collective-permute-start(f32[4,2,66,1]{3,2,0,1:T(8,128)S(1)} %get-tuple-element.67), channel_id=1, source_target_pairs={{1,0},{2,1},{3,2},{4,3},{5,4},{6,5},{7,6},{9,8},{10,9},{11,10},{12... | collective-permute-start | bytes 6344 | tf_op jit(solution)/shard_map/ppermute | solution.py:20
  253.3 7.4 %collective-permute-start.42 = (f32[4,2,66,1]{3,2,0,1:T(8,128)S(1)}, f32[4,2,66,1]{3,2,0,1:T(8,128)S(1)}, u32[]{:S(2)}, u32[]{:S(2)}) collective-permute-start(f32[4,2,66,1]{3,2,0,1:T(8,128)S(1)} %get-tuple-element.64), channel_id=1, source_target_pairs={{0,1},{1,2},{2,3},{3,4},{4,5},{5,6},{6,7},{8,9},{9,10},{10,11},{11... | collective-permute-start | bytes 6344 | tf_op jit(solution)/shard_map/ppermute | solution.py:19
  255.3 11.9 %collective-permute-start.43 = (f32[4,2,66,1]{3,2,0,1:T(8,128)S(1)}, f32[4,2,66,1]{3,2,0,1:T(8,128)S(1)}, u32[]{:S(2)}, u32[]{:S(2)}) collective-permute-start(f32[4,2,66,1]{3,2,0,1:T(8,128)S(1)} %get-tuple-element.65), channel_id=1, source_target_pairs={{1,0},{2,1},{3,2},{4,3},{5,4},{6,5},{7,6},{9,8},{10,9},{11,10},{12... | collective-permute-start | bytes 6344 | tf_op jit(solution)/shard_map/ppermute | solution.py:20
  276.1 7.4 %collective-permute-start.46 = (f32[4,2,66,1]{3,2,0,1:T(8,128)S(1)}, f32[4,2,66,1]{3,2,0,1:T(8,128)S(1)}, u32[]{:S(2)}, u32[]{:S(2)}) collective-permute-start(f32[4,2,66,1]{3,2,0,1:T(8,128)S(1)} %get-tuple-element.62), channel_id=1, source_target_pairs={{0,1},{1,2},{2,3},{3,4},{4,5},{5,6},{6,7},{8,9},{9,10},{10,11},{11... | collective-permute-start | bytes 6344 | tf_op jit(solution)/shard_map/ppermute | solution.py:19
  278.1 11.9 %collective-permute-start.47 = (f32[4,2,66,1]{3,2,0,1:T(8,128)S(1)}, f32[4,2,66,1]{3,2,0,1:T(8,128)S(1)}, u32[]{:S(2)}, u32[]{:S(2)}) collective-permute-start(f32[4,2,66,1]{3,2,0,1:T(8,128)S(1)} %get-tuple-element.63), channel_id=1, source_target_pairs={{1,0},{2,1},{3,2},{4,3},{5,4},{6,5},{7,6},{9,8},{10,9},{11,10},{12... | collective-permute-start | bytes 6344 | tf_op jit(solution)/shard_map/ppermute | solution.py:20
  299.0 7.4 %collective-permute-start.50 = (f32[4,2,66,1]{3,2,0,1:T(8,128)S(1)}, f32[4,2,66,1]{3,2,0,1:T(8,128)S(1)}, u32[]{:S(2)}, u32[]{:S(2)}) collective-permute-start(f32[4,2,66,1]{3,2,0,1:T(8,128)S(1)} %get-tuple-element.60), channel_id=1, source_target_pairs={{0,1},{1,2},{2,3},{3,4},{4,5},{5,6},{6,7},{8,9},{9,10},{10,11},{11... | collective-permute-start | bytes 6344 | tf_op jit(solution)/shard_map/ppermute | solution.py:19
  301.0 11.9 %collective-permute-start.51 = (f32[4,2,66,1]{3,2,0,1:T(8,128)S(1)}, f32[4,2,66,1]{3,2,0,1:T(8,128)S(1)}, u32[]{:S(2)}, u32[]{:S(2)}) collective-permute-start(f32[4,2,66,1]{3,2,0,1:T(8,128)S(1)} %get-tuple-element.61), channel_id=1, source_target_pairs={{1,0},{2,1},{3,2},{4,3},{5,4},{6,5},{7,6},{9,8},{10,9},{11,10},{12... | collective-permute-start | bytes 6344 | tf_op jit(solution)/shard_map/ppermute | solution.py:20
  322.2 7.2 %collective-permute-start.54 = (f32[4,2,66,1]{3,2,0,1:T(8,128)S(1)}, f32[4,2,66,1]{3,2,0,1:T(8,128)S(1)}, u32[]{:S(2)}, u32[]{:S(2)}) collective-permute-start(f32[4,2,66,1]{3,2,0,1:T(8,128)S(1)} %get-tuple-element.58), channel_id=1, source_target_pairs={{0,1},{1,2},{2,3},{3,4},{4,5},{5,6},{6,7},{8,9},{9,10},{10,11},{11... | collective-permute-start | bytes 6344 | tf_op jit(solution)/shard_map/ppermute | solution.py:19
  324.0 11.9 %collective-permute-start.55 = (f32[4,2,66,1]{3,2,0,1:T(8,128)S(1)}, f32[4,2,66,1]{3,2,0,1:T(8,128)S(1)}, u32[]{:S(2)}, u32[]{:S(2)}) collective-permute-start(f32[4,2,66,1]{3,2,0,1:T(8,128)S(1)} %get-tuple-element.59), channel_id=1, source_target_pairs={{1,0},{2,1},{3,2},{4,3},{5,4},{6,5},{7,6},{9,8},{10,9},{11,10},{12... | collective-permute-start | bytes 6344 | tf_op jit(solution)/shard_map/ppermute | solution.py:20
  345.9 7.4 %collective-permute-start.58 = (f32[4,2,66,1]{3,2,0,1:T(8,128)S(1)}, f32[4,2,66,1]{3,2,0,1:T(8,128)S(1)}, u32[]{:S(2)}, u32[]{:S(2)}) collective-permute-start(f32[4,2,66,1]{3,2,0,1:T(8,128)S(1)} %get-tuple-element.56), channel_id=1, source_target_pairs={{0,1},{1,2},{2,3},{3,4},{4,5},{5,6},{6,7},{8,9},{9,10},{10,11},{11... | collective-permute-start | bytes 6344 | tf_op jit(solution)/shard_map/ppermute | solution.py:19
  347.9 11.9 %collective-permute-start.59 = (f32[4,2,66,1]{3,2,0,1:T(8,128)S(1)}, f32[4,2,66,1]{3,2,0,1:T(8,128)S(1)}, u32[]{:S(2)}, u32[]{:S(2)}) collective-permute-start(f32[4,2,66,1]{3,2,0,1:T(8,128)S(1)} %get-tuple-element.57), channel_id=1, source_target_pairs={{1,0},{2,1},{3,2},{4,3},{5,4},{6,5},{7,6},{9,8},{10,9},{11,10},{12... | collective-permute-start | bytes 6344 | tf_op jit(solution)/shard_map/ppermute | solution.py:20
  369.5 7.4 %collective-permute-start.62 = (f32[4,2,66,1]{3,2,0,1:T(8,128)S(1)}, f32[4,2,66,1]{3,2,0,1:T(8,128)S(1)}, u32[]{:S(2)}, u32[]{:S(2)}) collective-permute-start(f32[4,2,66,1]{3,2,0,1:T(8,128)S(1)} %get-tuple-element.54), channel_id=1, source_target_pairs={{0,1},{1,2},{2,3},{3,4},{4,5},{5,6},{6,7},{8,9},{9,10},{10,11},{11... | collective-permute-start | bytes 6344 | tf_op jit(solution)/shard_map/ppermute | solution.py:19
  371.4 11.9 %collective-permute-start.63 = (f32[4,2,66,1]{3,2,0,1:T(8,128)S(1)}, f32[4,2,66,1]{3,2,0,1:T(8,128)S(1)}, u32[]{:S(2)}, u32[]{:S(2)}) collective-permute-start(f32[4,2,66,1]{3,2,0,1:T(8,128)S(1)} %get-tuple-element.55), channel_id=1, source_target_pairs={{1,0},{2,1},{3,2},{4,3},{5,4},{6,5},{7,6},{9,8},{10,9},{11,10},{12... | collective-permute-start | bytes 6344 | tf_op jit(solution)/shard_map/ppermute | solution.py:20
  392.4 7.4 %collective-permute-start.66 = (f32[4,2,66,1]{3,2,1,0:T(8,128)S(1)}, f32[4,2,66,1]{3,2,1,0:T(8,128)S(1)}, u32[]{:S(2)}, u32[]{:S(2)}) collective-permute-start(f32[4,2,66,1]{3,2,1,0:T(8,128)S(1)} %get-tuple-element.52), channel_id=1, source_target_pairs={{0,1},{1,2},{2,3},{3,4},{4,5},{5,6},{6,7},{8,9},{9,10},{10,11},{11... | collective-permute-start | bytes 6344 | tf_op jit(solution)/shard_map/ppermute | solution.py:19
  394.4 11.9 %collective-permute-start.67 = (f32[4,2,66,1]{3,2,1,0:T(8,128)S(1)}, f32[4,2,66,1]{3,2,1,0:T(8,128)S(1)}, u32[]{:S(2)}, u32[]{:S(2)}) collective-permute-start(f32[4,2,66,1]{3,2,1,0:T(8,128)S(1)} %get-tuple-element.53), channel_id=1, source_target_pairs={{1,0},{2,1},{3,2},{4,3},{5,4},{6,5},{7,6},{9,8},{10,9},{11,10},{12... | collective-permute-start | bytes 6344 | tf_op jit(solution)/shard_map/ppermute | solution.py:20
  (44 other events, 213.2 us)
where the time goes:
time: 497 us; the launch traced here: 494 us
  waiting for transfers between devices  229 us (46%)
  starting transfers between devices  152 us (31%)
  blocking collectives  81.4 us (16%)
  other arithmetic  21.1 us (4%)
  local copies, waits for them, and re-layouts  7.62 us (2%)
    ppermute x34, waiting for transfers between devices, extended(): after = lax.ppermute(first, axis, down)  161 us
    ppermute x34, starting transfers between devices, extended(): before = lax.ppermute(last, axis, up)  94 us
    psum x1, blocking collectives, body(): gram = lax.psum(placed, ('probe', 'gx', 'gy')) / total_cells  74.6 us
    ppermute x34, waiting for transfers between devices, extended(): before = lax.ppermute(last, axis, up)  67.2 us
    ppermute x34, starting transfers between devices, extended(): after = lax.ppermute(first, axis, down)  58.2 us
  transfers between devices with their start and end apart: 68, of which 50 were waited for; matrix products, arithmetic and copies ran while one was open for 0% of the time, Pallas kernels for 0%

commit v1 on v0

--- a/solution.py
+++ b/solution.py
@@ -114,7 +114,7 @@
     placed = lax.dynamic_update_slice(
         jnp.zeros((probe_total, probe_total), jnp.float32), partial_rows, (start, 0)
     )
-    gram = lax.psum(placed, ("probe", "gx", "gy")) / total_cells
+    gram = jnp.sum(lax.all_gather(placed, ("probe", "gx", "gy")), axis=0) / total_cells
     lower = jnp.linalg.cholesky(gram)
     solved = jax.scipy.linalg.solve_triangular(lower, flat_images, lower=True)
     factor = lax.dynamic_slice_in_dim(solved, start, probes.shape[0], 0).reshape(probes.shape)

time: 497 us -> 1050 us (2.11); the launches traced: 494 us -> 1030 us
  blocking collectives: 81.4 us -> 616 us
    all_gather x0 -> x1, blocking collectives: none -> 609 us  [body(): lax.all_gather(placed, ('probe', 'gx', 'gy'))]
    psum x1 -> x0, blocking collectives: 74.6 us -> none  [body(): gram = lax.psum(placed, ('probe', 'gx', 'gy')) / total_cells]
where the time goes in v1:
time: 1050 us; the launch traced here: 1030 us
  blocking collectives  616 us (59%)
  waiting for transfers between devices  229 us (22%)
  starting transfers between devices  152 us (14%)
  other arithmetic  21.3 us (2%)
    all_gather x1, blocking collectives, body(): lax.all_gather(placed, ('probe', 'gx', 'gy'))  609 us
    ppermute x34, waiting for transfers between devices, extended(): after = lax.ppermute(first, axis, down)  161 us
    ppermute x34, starting transfers between devices, extended(): before = lax.ppermute(last, axis, up)  94 us
    ppermute x34, waiting for transfers between devices, extended(): before = lax.ppermute(last, axis, up)  67.2 us
    ppermute x34, starting transfers between devices, extended(): after = lax.ppermute(first, axis, down)  58.2 us
  transfers between devices with their start and end apart: 68, of which 50 were waited for; matrix products, arithmetic and copies ran while one was open for 0% of the time, Pallas kernels for 0%

profile of v1, /device:TPU:1, one launch (start us, length us, event | category | flops | bytes accessed | tf_op | source)
XLA Modules:
  0.0 1028.8 jit_solution(18068588053169233271)
XLA Ops:
  1.3 5.1 collective-permute-start
  18.7 4.9 collective-permute-start.4
  34.0 4.1 collective-permute-done.6
  38.1 9.6 collective-permute-done.7
  59.9 4.1 collective-permute-done.10
  64.0 9.8 collective-permute-done.11
  86.4 4.1 collective-permute-done.14
  90.5 9.8 collective-permute-done.15
  101.4 4.5 collective-permute-start.16
  117.6 6.5 collective-permute-done.19
  136.6 4.1 collective-permute-done.22
  140.7 6.5 collective-permute-done.23
  148.4 4.2 collective-permute-start.24
  161.0 4.1 collective-permute-done.26
  165.1 6.5 collective-permute-done.27
  189.4 6.5 collective-permute-done.31
  209.4 4.1 collective-permute-done.34
  213.5 6.5 collective-permute-done.35
  233.6 4.1 collective-permute-done.38
  237.7 6.5 collective-permute-done.39
  256.6 4.1 collective-permute-done.42
  260.7 6.5 collective-permute-done.43
  279.4 4.1 collective-permute-done.46
  283.5 6.5 collective-permute-done.47
  302.3 4.1 collective-permute-done.50
  306.4 6.5 collective-permute-done.51
  329.4 6.5 collective-permute-done.55
  353.3 6.5 collective-permute-done.59
  376.8 6.5 collective-permute-done.63
  399.8 6.5 collective-permute-done.67
  407.4 6.8 all_gather.9
  414.9 609.0 %all_gather.11 = f32[256,8,8]{2,1,0:T(8,128)S(1)} all-gather(f32[1,8,8]{2,1,0:T(8,128)S(1)} %fusion), channel_id=1, replica_groups=mesh['probe'=2,'gx'=16,'gy'=8] {'probe','gx','gy'}, dimensions={0}, use_global_device_ids=true | all-gather | bytes 65792 | tf_op jit(solution)/shard_map/all_gather | solution.py:117
  (274 shorter events, 237.5 us)
Async XLA Ops:
  1.3 7.1 collective-permute-start
  18.7 6.8 collective-permute-start.4
  28.7 9.4 collective-permute-start.6
  32.7 15.0 %collective-permute-start.7 = (f32[4,2,66,1]{3,2,0,1:T(8,128)S(1)}, f32[4,2,66,1]{3,2,0,1:T(8,128)S(1)}, u32[]{:S(2)}, u32[]{:S(2)}) collective-permute-start(f32[4,2,66,1]{3,2,0,1:T(8,128)S(1)} %get-tuple-element.83), channel_id=1, source_target_pairs={{1,0},{2,1},{3,2},{4,3},{5,4},{6,5},{7,6},{9,8},{10,9},{11,10},{12... | collective-permute-start | bytes 6344 | tf_op jit(solution)/shard_map/ppermute | solution.py:20
  58.6 15.2 %collective-permute-start.11 = (f32[4,2,66,1]{3,2,0,1:T(8,128)S(1)}, f32[4,2,66,1]{3,2,0,1:T(8,128)S(1)}, u32[]{:S(2)}, u32[]{:S(2)}) collective-permute-start(f32[4,2,66,1]{3,2,0,1:T(8,128)S(1)} %get-tuple-element.81), channel_id=1, source_target_pairs={{1,0},{2,1},{3,2},{4,3},{5,4},{6,5},{7,6},{9,8},{10,9},{11,10},{12... | collective-permute-start | bytes 6344 | tf_op jit(solution)/shard_map/ppermute | solution.py:20
  83.7 6.7 collective-permute-start.14
  85.1 15.2 %collective-permute-start.15 = (f32[4,2,66,1]{3,2,0,1:T(8,128)S(1)}, f32[4,2,66,1]{3,2,0,1:T(8,128)S(1)}, u32[]{:S(2)}, u32[]{:S(2)}) collective-permute-start(f32[4,2,66,1]{3,2,0,1:T(8,128)S(1)} %get-tuple-element.79), channel_id=1, source_target_pairs={{1,0},{2,1},{3,2},{4,3},{5,4},{6,5},{7,6},{9,8},{10,9},{11,10},{12... | collective-permute-start | bytes 6344 | tf_op jit(solution)/shard_map/ppermute | solution.py:20
  112.3 11.8 %collective-permute-start.19 = (f32[4,2,66,1]{3,2,0,1:T(8,128)S(1)}, f32[4,2,66,1]{3,2,0,1:T(8,128)S(1)}, u32[]{:S(2)}, u32[]{:S(2)}) collective-permute-start(f32[4,2,66,1]{3,2,0,1:T(8,128)S(1)} %get-tuple-element.77), channel_id=1, source_target_pairs={{1,0},{2,1},{3,2},{4,3},{5,4},{6,5},{7,6},{9,8},{10,9},{11,10},{12... | collective-permute-start | bytes 6344 | tf_op jit(solution)/shard_map/ppermute | solution.py:20
  133.3 7.4 collective-permute-start.22
  135.3 11.9 %collective-permute-start.23 = (f32[4,2,66,1]{3,2,0,1:T(8,128)S(1)}, f32[4,2,66,1]{3,2,0,1:T(8,128)S(1)}, u32[]{:S(2)}, u32[]{:S(2)}) collective-permute-start(f32[4,2,66,1]{3,2,0,1:T(8,128)S(1)} %get-tuple-element.75), channel_id=1, source_target_pairs={{1,0},{2,1},{3,2},{4,3},{5,4},{6,5},{7,6},{9,8},{10,9},{11,10},{12... | collective-permute-start | bytes 6344 | tf_op jit(solution)/shard_map/ppermute | solution.py:20
  157.7 7.4 collective-permute-start.26
  159.7 11.9 %collective-permute-start.27 = (f32[4,2,66,1]{3,2,0,1:T(8,128)S(1)}, f32[4,2,66,1]{3,2,0,1:T(8,128)S(1)}, u32[]{:S(2)}, u32[]{:S(2)}) collective-permute-start(f32[4,2,66,1]{3,2,0,1:T(8,128)S(1)} %get-tuple-element.73), channel_id=1, source_target_pairs={{1,0},{2,1},{3,2},{4,3},{5,4},{6,5},{7,6},{9,8},{10,9},{11,10},{12... | collective-permute-start | bytes 6344 | tf_op jit(solution)/shard_map/ppermute | solution.py:20
  182.0 7.4 collective-permute-start.30
  184.0 11.9 %collective-permute-start.31 = (f32[4,2,66,1]{3,2,0,1:T(8,128)S(1)}, f32[4,2,66,1]{3,2,0,1:T(8,128)S(1)}, u32[]{:S(2)}, u32[]{:S(2)}) collective-permute-start(f32[4,2,66,1]{3,2,0,1:T(8,128)S(1)} %get-tuple-element.71), channel_id=1, source_target_pairs={{1,0},{2,1},{3,2},{4,3},{5,4},{6,5},{7,6},{9,8},{10,9},{11,10},{12... | collective-permute-start | bytes 6344 | tf_op jit(solution)/shard_map/ppermute | solution.py:20
  206.1 7.4 collective-permute-start.34
  208.1 11.9 %collective-permute-start.35 = (f32[4,2,66,1]{3,2,0,1:T(8,128)S(1)}, f32[4,2,66,1]{3,2,0,1:T(8,128)S(1)}, u32[]{:S(2)}, u32[]{:S(2)}) collective-permute-start(f32[4,2,66,1]{3,2,0,1:T(8,128)S(1)} %get-tuple-element.69), channel_id=1, source_target_pairs={{1,0},{2,1},{3,2},{4,3},{5,4},{6,5},{7,6},{9,8},{10,9},{11,10},{12... | collective-permute-start | bytes 6344 | tf_op jit(solution)/shard_map/ppermute | solution.py:20
  230.3 7.4 collective-permute-start.38
  232.3 11.9 %collective-permute-start.39 = (f32[4,2,66,1]{3,2,0,1:T(8,128)S(1)}, f32[4,2,66,1]{3,2,0,1:T(8,128)S(1)}, u32[]{:S(2)}, u32[]{:S(2)}) collective-permute-start(f32[4,2,66,1]{3,2,0,1:T(8,128)S(1)} %get-tuple-element.67), channel_id=1, source_target_pairs={{1,0},{2,1},{3,2},{4,3},{5,4},{6,5},{7,6},{9,8},{10,9},{11,10},{12... | collective-permute-start | bytes 6344 | tf_op jit(solution)/shard_map/ppermute | solution.py:20
  253.3 7.4 collective-permute-start.42
  255.3 11.9 %collective-permute-start.43 = (f32[4,2,66,1]{3,2,0,1:T(8,128)S(1)}, f32[4,2,66,1]{3,2,0,1:T(8,128)S(1)}, u32[]{:S(2)}, u32[]{:S(2)}) collective-permute-start(f32[4,2,66,1]{3,2,0,1:T(8,128)S(1)} %get-tuple-element.65), channel_id=1, source_target_pairs={{1,0},{2,1},{3,2},{4,3},{5,4},{6,5},{7,6},{9,8},{10,9},{11,10},{12... | collective-permute-start | bytes 6344 | tf_op jit(solution)/shard_map/ppermute | solution.py:20
  276.1 7.4 collective-permute-start.46
  278.1 11.9 %collective-permute-start.47 = (f32[4,2,66,1]{3,2,0,1:T(8,128)S(1)}, f32[4,2,66,1]{3,2,0,1:T(8,128)S(1)}, u32[]{:S(2)}, u32[]{:S(2)}) collective-permute-start(f32[4,2,66,1]{3,2,0,1:T(8,128)S(1)} %get-tuple-element.63), channel_id=1, source_target_pairs={{1,0},{2,1},{3,2},{4,3},{5,4},{6,5},{7,6},{9,8},{10,9},{11,10},{12... | collective-permute-start | bytes 6344 | tf_op jit(solution)/shard_map/ppermute | solution.py:20
  299.0 7.4 collective-permute-start.50
  301.0 11.9 %collective-permute-start.51 = (f32[4,2,66,1]{3,2,0,1:T(8,128)S(1)}, f32[4,2,66,1]{3,2,0,1:T(8,128)S(1)}, u32[]{:S(2)}, u32[]{:S(2)}) collective-permute-start(f32[4,2,66,1]{3,2,0,1:T(8,128)S(1)} %get-tuple-element.61), channel_id=1, source_target_pairs={{1,0},{2,1},{3,2},{4,3},{5,4},{6,5},{7,6},{9,8},{10,9},{11,10},{12... | collective-permute-start | bytes 6344 | tf_op jit(solution)/shard_map/ppermute | solution.py:20
  322.2 7.2 collective-permute-start.54
  324.0 11.9 %collective-permute-start.55 = (f32[4,2,66,1]{3,2,0,1:T(8,128)S(1)}, f32[4,2,66,1]{3,2,0,1:T(8,128)S(1)}, u32[]{:S(2)}, u32[]{:S(2)}) collective-permute-start(f32[4,2,66,1]{3,2,0,1:T(8,128)S(1)} %get-tuple-element.59), channel_id=1, source_target_pairs={{1,0},{2,1},{3,2},{4,3},{5,4},{6,5},{7,6},{9,8},{10,9},{11,10},{12... | collective-permute-start | bytes 6344 | tf_op jit(solution)/shard_map/ppermute | solution.py:20
  345.9 7.4 collective-permute-start.58
  347.9 11.9 %collective-permute-start.59 = (f32[4,2,66,1]{3,2,0,1:T(8,128)S(1)}, f32[4,2,66,1]{3,2,0,1:T(8,128)S(1)}, u32[]{:S(2)}, u32[]{:S(2)}) collective-permute-start(f32[4,2,66,1]{3,2,0,1:T(8,128)S(1)} %get-tuple-element.57), channel_id=1, source_target_pairs={{1,0},{2,1},{3,2},{4,3},{5,4},{6,5},{7,6},{9,8},{10,9},{11,10},{12... | collective-permute-start | bytes 6344 | tf_op jit(solution)/shard_map/ppermute | solution.py:20
  369.5 7.4 collective-permute-start.62
  371.4 11.9 %collective-permute-start.63 = (f32[4,2,66,1]{3,2,0,1:T(8,128)S(1)}, f32[4,2,66,1]{3,2,0,1:T(8,128)S(1)}, u32[]{:S(2)}, u32[]{:S(2)}) collective-permute-start(f32[4,2,66,1]{3,2,0,1:T(8,128)S(1)} %get-tuple-element.55), channel_id=1, source_target_pairs={{1,0},{2,1},{3,2},{4,3},{5,4},{6,5},{7,6},{9,8},{10,9},{11,10},{12... | collective-permute-start | bytes 6344 | tf_op jit(solution)/shard_map/ppermute | solution.py:20
  392.4 7.4 collective-permute-start.66
  394.4 11.9 %collective-permute-start.67 = (f32[4,2,66,1]{3,2,1,0:T(8,128)S(1)}, f32[4,2,66,1]{3,2,1,0:T(8,128)S(1)}, u32[]{:S(2)}, u32[]{:S(2)}) collective-permute-start(f32[4,2,66,1]{3,2,1,0:T(8,128)S(1)} %get-tuple-element.53), channel_id=1, source_target_pairs={{1,0},{2,1},{3,2},{4,3},{5,4},{6,5},{7,6},{9,8},{10,9},{11,10},{12... | collective-permute-start | bytes 6344 | tf_op jit(solution)/shard_map/ppermute | solution.py:20
  (44 other events, 213.2 us)
